TPU v7x, 32 devices: a whole 2x2x4 slice. The times are simulated.
32 devices in a mesh: dom: 2 (over core), gx: 4 (over y, x), gy: 4 (over z).
Axes of the slice: x: 2, y: 2, z: 4, core: 2. Of those that a mesh axis runs over, the one named last changes fastest.
Arguments:
- velocity: float32 [2, 3, 64, 32, 128], P('dom', None, 'gx', 'gy'), may hold values from -5 to 5
- fringe_start: int32 [1], replicated, may hold values from 0 to 63
Outputs:
- velocity_out: float32 [2, 3, 64, 32, 128], P('dom', None, 'gx', 'gy')
- spectrum: float32 [2, 128, 64, 32], P(None, ('dom', 'gx'), 'gy')
All inputs are finite; a program needn't handle non-finite values.
Results may differ from a plain program's by a relative error of at most 0.000084.
Values sent between devices are 32-bit elements; how exact they have to be, the bound alone decides.
A program may use at most 64 MiB of HBM per device.

v0:
```python
import math

import jax
import jax.numpy as jnp
from jax import lax
from jax.sharding import PartitionSpec as P

time_step = 0.1
fringe_rate = 1.0
smag_coef = 0.03
base_visc = 0.02
strain_floor = 0.25


def with_halo(block, sides, width):
    for axis, dim in sides:
        count = lax.axis_size(axis)
        forward = [(i, i + 1) for i in range(count - 1)]
        forward.append((count - 1, 0))
        backward = [(target, source) for source, target in forward]
        low = lax.ppermute(
            lax.slice_in_dim(block, block.shape[dim] - width, None, axis=dim), axis, forward
        )
        high = lax.ppermute(lax.slice_in_dim(block, 0, width, axis=dim), axis, backward)
        block = jnp.concatenate([low, block, high], axis=dim)
    return block


def from_behind(shard, axis, by):
    peers = lax.axis_size(axis)
    pairs = [(i, i + by) for i in range(peers) if 0 <= i + by < peers]
    return lax.ppermute(shard, axis, pairs)


def combine(center, x_plus, x_minus, y_plus, y_minus, z_plus, z_minus, inflow, fringe_ramp):
    grad_x = 0.5 * (x_plus - x_minus)
    grad_y = 0.5 * (y_plus - y_minus)
    grad_z = 0.5 * (z_plus - z_minus)
    gradients = (grad_x, grad_y, grad_z)
    strain = jnp.zeros_like(center[0])
    for comp_a in range(3):
        for comp_b in range(3):
            sym_part = 0.5 * (gradients[comp_b][comp_a] + gradients[comp_a][comp_b])
            strain = strain + sym_part * sym_part
    eddy_visc = base_visc + smag_coef * jnp.sqrt(2.0 * strain + strain_floor)
    advection = center[0] * grad_x + center[1] * grad_y + center[2] * grad_z
    laplace_term = x_plus + x_minus + y_plus + y_minus + z_plus + z_minus - 6.0 * center
    return -advection + eddy_visc * laplace_term + fringe_ramp * (inflow - center)


def ramp_values(fringe_start, x_cells, fringe_len, total_len):
    offset = (x_cells - fringe_start[0] + total_len) % total_len
    inside = offset < fringe_len
    sine_part = jnp.sin((offset.astype(jnp.float32) + 0.5) * (math.pi / fringe_len))
    return jnp.where(inside, fringe_rate * sine_part * sine_part, 0.0)


def trim_margin(field, margin):
    if margin == 0:
        return field
    return field[:, margin:-margin, margin:-margin, :]


def extend(field, width):
    return with_halo(field, (("gx", 1), ("gy", 2)), width)


def tendency(field, inflow, fringe_ramp):
    padded = jnp.pad(field, ((0, 0), (0, 0), (0, 0), (1, 1)))
    return combine(
        field[:, 1:-1, 1:-1, :],
        field[:, 2:, 1:-1, :],
        field[:, :-2, 1:-1, :],
        field[:, 1:-1, 2:, :],
        field[:, 1:-1, :-2, :],
        padded[:, 1:-1, 1:-1, 2:],
        padded[:, 1:-1, 1:-1, :-2],
        inflow,
        fringe_ramp,
    )


def partner_half(values):
    return from_behind(values, "dom", -1)


def dft_tables(length):
    positions = jnp.arange(length, dtype=jnp.int32)
    phase = (positions[:, None] * positions[None, :] % length).astype(jnp.float32) * (
        2.0 * math.pi / length
    )
    factor = 1.0 / math.sqrt(length)
    return (jnp.cos(phase) * factor, jnp.sin(phase) * factor)


def on_device(velocity, fringe_start):
    own_field = velocity[0]
    cells_x = own_field.shape[1]
    cells_y = own_field.shape[2]
    levels_z = own_field.shape[3]
    tiles_x = lax.axis_size("gx")
    total_x = cells_x * tiles_x
    total_y = cells_y * lax.axis_size("gy")
    fringe_len = min(8 * cells_x, total_x // 2)
    is_farm = lax.axis_index("dom") == 1
    inflow = from_behind(own_field, "dom", 1)
    margin = 0
    x_cells = (
        lax.axis_index("gx") * cells_x
        - margin
        + total_x
        + jnp.arange(cells_x + 2 * margin, dtype=jnp.int32)
    ) % total_x
    ramp_full = (
        ramp_values(fringe_start, x_cells, fringe_len, total_x) * is_farm.astype(jnp.float32)
    ).reshape(-1, 1, 1)

    def advance(current, depth_now):
        current = extend(current, 1)
        depth_now = 1
        cut = margin - depth_now + 1
        rates = tendency(current, trim_margin(inflow, cut), ramp_full)
        return (trim_margin(current, 1), depth_now - 1, rates)

    prior, depth, rates = advance(own_field, margin)
    section_one = trim_margin(own_field, margin - depth) + time_step * rates
    prior, depth, rates = advance(section_one, depth)
    section_two = 0.75 * trim_margin(own_field, margin - depth) + 0.25 * (prior + time_step * rates)
    prior, depth, rates = advance(section_two, depth)
    section_three = 1.0 / 3.0 * trim_margin(own_field, margin - depth) + 2.0 / 3.0 * (
        prior + time_step * rates
    )
    field_out = trim_margin(section_three, depth)
    beside_all = extend(section_three, 1)
    padded = jnp.pad(beside_all[2], ((0, 0), (0, 0), (1, 1)))
    divergence = (
        0.5 * (beside_all[0][2:, 1:-1] - beside_all[0][:-2, 1:-1])
        + 0.5 * (beside_all[1][1:-1, 2:] - beside_all[1][1:-1, :-2])
        + 0.5 * (padded[1:-1, 1:-1, 2:] - padded[1:-1, 1:-1, :-2])
    )
    levels_out = levels_z // (2 * tiles_x)
    tile_block = divergence.reshape(cells_x, cells_y, 2, tiles_x, levels_out)
    highest = lax.Precision.HIGHEST
    cos_table_x, sin_table_x = dft_tables(total_x)
    cos_table_y, sin_table_y = dft_tables(total_y)
    shard_piece = lax.all_to_all(tile_block, "gx", split_axis=3, concat_axis=0, tiled=True)
    real_part = jnp.einsum("xyhgc,xk->yhck", shard_piece, cos_table_x, precision=highest)
    imag_part = -jnp.einsum("xyhgc,xk->yhck", shard_piece, sin_table_x, precision=highest)
    real_part, imag_part = (real_part, imag_part)
    real_in = lax.all_to_all(real_part, "gy", split_axis=3, concat_axis=0, tiled=True)
    imag_in = lax.all_to_all(imag_part, "gy", split_axis=3, concat_axis=0, tiled=True)
    real_out = jnp.einsum("yhck,yj->hckj", real_in, cos_table_y, precision=highest) + jnp.einsum(
        "yhck,yj->hckj", imag_in, sin_table_y, precision=highest
    )
    imag_out = jnp.einsum("yhck,yj->hckj", imag_in, cos_table_y, precision=highest) - jnp.einsum(
        "yhck,yj->hckj", real_in, sin_table_y, precision=highest
    )
    packed = jnp.stack([real_out, imag_out])
    received = partner_half(packed[:, 0])
    spectrum = jnp.where(is_farm, packed[:, 1], received)
    return (field_out[None], spectrum)


def solution(mesh):
    in_specs = (P("dom", None, "gx", "gy", None), P())
    out_specs = (P("dom", None, "gx", "gy", None), P(None, ("dom", "gx"), "gy", None))
    return jax.shard_map(
        on_device, mesh=mesh, in_specs=in_specs, out_specs=out_specs, check_vma=False
    )
```

profile of v0, /device:TPU:1, one launch (start us, length us, event | category | flops | bytes accessed | tf_op | source)
XLA Modules:
  0.0 97.5 jit_solution(3738386466762272242)
XLA Ops:
  0.6 1.3 %collective-permute-start.4 = (f32[3,16,8,128]{3,2,1,0:T(8,128)}, f32[3,16,8,128]{3,2,1,0:T(8,128)S(1)}, u32[]{:S(2)}, u32[]{:S(2)}) collective-permute-start(f32[3,16,8,128]{3,2,1,0:T(8,128)} %bitcast.99), channel_id=1, source_target_pairs={{0,16},{1,17},{2,18},{3,19},{4,20},{5,21},{6,22},{7,23},{8,24},{9,... | collective-permute-start | bytes 589832 | tf_op jit(solution)/shard_map/ppermute | solution.py:32
  2.7 3.0 %collective-permute-start = (f32[3,1,8,128]{3,2,1,0:T(8,128)S(1)}, f32[3,1,8,128]{3,2,1,0:T(8,128)S(1)}, u32[]{:S(2)}, u32[]{:S(2)}) collective-permute-start(f32[3,1,8,128]{3,2,1,0:T(8,128)S(1)} %get-tuple-element.35), channel_id=1, source_target_pairs={{4,0},{8,4},{12,8},{0,12},{5,1},{9,5},{13,9},{1,13},{6,2},{10,6},{... | collective-permute-start | bytes 36872 | tf_op jit(solution)/shard_map/ppermute | solution.py:24
  7.3 1.8 %collective-permute-done.1 = f32[3,1,8,128]{3,2,1,0:T(8,128)S(1)} collective-permute-done((f32[3,1,8,128]{3,2,1,0:T(8,128)S(1)}, f32[3,1,8,128]{3,2,1,0:T(8,128)S(1)}, u32[]{:S(2)}, u32[]{:S(2)}) %collective-permute-start.1) | collective-permute-done | bytes 12320 | tf_op jit(solution)/shard_map/ppermute | solution.py:21
  9.1 3.4 %collective-permute-start.2 = (f32[3,18,1,128]{3,2,1,0:T(1,128)S(1)}, f32[3,18,1,128]{3,2,1,0:T(1,128)S(1)}, u32[]{:S(2)}, u32[]{:S(2)}) collective-permute-start(f32[3,18,1,128]{3,2,1,0:T(1,128)S(1)} %get-tuple-element.18), channel_id=1, source_target_pairs={{1,0},{2,1},{3,2},{0,3},{5,4},{6,5},{7,6},{4,7},{9,8},{10,9},{11,1... | collective-permute-start | bytes 82952 | tf_op jit(solution)/shard_map/ppermute | solution.py:24
  13.5 3.8 %collective-permute-done.3 = f32[3,18,1,128]{3,2,1,0:T(1,128)S(1)} collective-permute-done((f32[3,18,1,128]{3,2,1,0:T(1,128)S(1)}, f32[3,18,1,128]{3,2,1,0:T(1,128)S(1)}, u32[]{:S(2)}, u32[]{:S(2)}) %collective-permute-start.3) | collective-permute-done | bytes 27680 | tf_op jit(solution)/shard_map/ppermute | solution.py:21
  21.0 1.2 %collective-permute-done.6 = f32[3,1,8,128]{3,2,1,0:T(8,128)S(1)} collective-permute-done((f32[3,1,8,128]{3,2,1,0:T(8,128)S(1)}, f32[3,1,8,128]{3,2,1,0:T(8,128)S(1)}, u32[]{:S(2)}, u32[]{:S(2)}) %collective-permute-start.6) | collective-permute-done | bytes 12320 | tf_op jit(solution)/shard_map/ppermute | solution.py:21
  22.3 1.5 %collective-permute-start.8 = (f32[3,18,1,128]{3,2,1,0:T(1,128)S(1)}, f32[3,18,1,128]{3,2,1,0:T(1,128)S(1)}, u32[]{:S(2)}, u32[]{:S(2)}) collective-permute-start(f32[3,18,1,128]{3,2,1,0:T(1,128)S(1)} %get-tuple-element.13), channel_id=1, source_target_pairs={{0,1},{1,2},{2,3},{3,0},{4,5},{5,6},{6,7},{7,4},{8,9},{9,10},{10,1... | collective-permute-start | bytes 82952 | tf_op jit(solution)/shard_map/ppermute | solution.py:21
  23.7 1.2 %collective-permute-done.7 = f32[3,18,1,128]{3,2,1,0:T(1,128)S(1)} collective-permute-done((f32[3,18,1,128]{3,2,1,0:T(1,128)S(1)}, f32[3,18,1,128]{3,2,1,0:T(1,128)S(1)}, u32[]{:S(2)}, u32[]{:S(2)}) %collective-permute-start.7) | collective-permute-done | bytes 27680 | tf_op jit(solution)/shard_map/ppermute | solution.py:24
  25.0 1.9 %collective-permute-done.8 = f32[3,18,1,128]{3,2,1,0:T(1,128)S(1)} collective-permute-done((f32[3,18,1,128]{3,2,1,0:T(1,128)S(1)}, f32[3,18,1,128]{3,2,1,0:T(1,128)S(1)}, u32[]{:S(2)}, u32[]{:S(2)}) %collective-permute-start.8) | collective-permute-done | bytes 27680 | tf_op jit(solution)/shard_map/ppermute | solution.py:21
  28.3 2.1 %collective-permute-start.9 = (f32[3,1,8,128]{3,2,1,0:T(8,128)S(1)}, f32[3,1,8,128]{3,2,1,0:T(8,128)S(1)}, u32[]{:S(2)}, u32[]{:S(2)}) collective-permute-start(f32[3,1,8,128]{3,2,1,0:T(8,128)S(1)} %get-tuple-element.25), channel_id=1, source_target_pairs={{4,0},{8,4},{12,8},{0,12},{5,1},{9,5},{13,9},{1,13},{6,2},{10,6},{... | collective-permute-start | bytes 36872 | tf_op jit(solution)/shard_map/ppermute | solution.py:24
  31.8 1.2 %collective-permute-start.12 = (f32[3,18,1,128]{3,2,1,0:T(1,128)S(1)}, f32[3,18,1,128]{3,2,1,0:T(1,128)S(1)}, u32[]{:S(2)}, u32[]{:S(2)}) collective-permute-start(f32[3,18,1,128]{3,2,1,0:T(1,128)S(1)} %get-tuple-element.9), channel_id=1, source_target_pairs={{0,1},{1,2},{2,3},{3,0},{4,5},{5,6},{6,7},{7,4},{8,9},{9,10},{10,1... | collective-permute-start | bytes 82952 | tf_op jit(solution)/shard_map/ppermute | solution.py:21
  33.1 1.2 %collective-permute-done.11 = f32[3,18,1,128]{3,2,1,0:T(1,128)S(1)} collective-permute-done((f32[3,18,1,128]{3,2,1,0:T(1,128)S(1)}, f32[3,18,1,128]{3,2,1,0:T(1,128)S(1)}, u32[]{:S(2)}, u32[]{:S(2)}) %collective-permute-start.11) | collective-permute-done | bytes 27680 | tf_op jit(solution)/shard_map/ppermute | solution.py:24
  34.3 2.0 %collective-permute-done.12 = f32[3,18,1,128]{3,2,1,0:T(1,128)S(1)} collective-permute-done((f32[3,18,1,128]{3,2,1,0:T(1,128)S(1)}, f32[3,18,1,128]{3,2,1,0:T(1,128)S(1)}, u32[]{:S(2)}, u32[]{:S(2)}) %collective-permute-start.12) | collective-permute-done | bytes 27680 | tf_op jit(solution)/shard_map/ppermute | solution.py:21
  37.5 1.4 %collective-permute-start.13 = (f32[3,1,8,128]{3,2,1,0:T(8,128)S(1)}, f32[3,1,8,128]{3,2,1,0:T(8,128)S(1)}, u32[]{:S(2)}, u32[]{:S(2)}) collective-permute-start(f32[3,1,8,128]{3,2,1,0:T(8,128)S(1)} %get-tuple-element.19), channel_id=1, source_target_pairs={{0,4},{4,8},{8,12},{12,0},{1,5},{5,9},{9,13},{13,1},{2,6},{6,10},{... | collective-permute-start | bytes 36872 | tf_op jit(solution)/shard_map/ppermute | solution.py:21
  41.6 3.3 %collective-permute-start.16 = (f32[3,18,1,128]{3,2,1,0:T(1,128)S(1)}, f32[3,18,1,128]{3,2,1,0:T(1,128)S(1)}, u32[]{:S(2)}, u32[]{:S(2)}) collective-permute-start(f32[3,18,1,128]{3,2,1,0:T(1,128)S(1)} %get-tuple-element.6), channel_id=1, source_target_pairs={{1,0},{2,1},{3,2},{0,3},{5,4},{6,5},{7,6},{4,7},{9,8},{10,9},{11,1... | collective-permute-start | bytes 82952 | tf_op jit(solution)/shard_map/ppermute | solution.py:24
  44.9 1.2 %collective-permute-done.15 = f32[3,18,1,128]{3,2,1,0:T(1,128)S(1)} collective-permute-done((f32[3,18,1,128]{3,2,1,0:T(1,128)S(1)}, f32[3,18,1,128]{3,2,1,0:T(1,128)S(1)}, u32[]{:S(2)}, u32[]{:S(2)}) %collective-permute-start.15) | collective-permute-done | bytes 27680 | tf_op jit(solution)/shard_map/ppermute | solution.py:21
  47.3 6.7 %all_to_all.51 = f32[4,1,4096]{2,1,0:T(1,128)S(1)} all-to-all(f32[4,1,4096]{2,1,0:T(1,128)S(1)} %reshape.74), channel_id=1, replica_groups=mesh['dom'=2,'gx'=4,'gy'=4] {'gx'}, dimensions={0} | all-to-all | bytes 131072 | tf_op jit(solution)/shard_map/all_to_all | solution.py:146
  57.0 1.4 %reshape.78 = f32[4,1,4096]{2,1,0:T(1,128)} reshape(f32[64,8,2,16]{3,2,1,0:T(2,128)S(1)} %bitcast.105) | data formatting | bytes 131072
  58.4 4.5 %all-to-all-start.1 = ((f32[4,1,4096]{2,1,0:T(1,128)}), f32[4,1,4096]{2,1,0:T(1,128)S(1)}, u32[]{:S(2)}, u32[]{:S(2)}) async-start(f32[4,1,4096]{2,1,0:T(1,128)} %reshape.78), calls=%async_computation.1 | async-start | bytes 131072 | tf_op jit(solution)/shard_map/all_to_all | solution.py:150
  63.7 1.4 %reshape.76 = f32[4,1,4096]{2,1,0:T(1,128)} reshape(f32[64,8,2,16]{3,2,1,0:T(2,128)S(1)} %bitcast.106) | data formatting | bytes 131072
  65.1 2.4 %all-to-all-done.1 = f32[4,1,4096]{2,1,0:T(1,128)S(1)} async-done(((f32[4,1,4096]{2,1,0:T(1,128)}), f32[4,1,4096]{2,1,0:T(1,128)S(1)}, u32[]{:S(2)}, u32[]{:S(2)}) %all-to-all-start.1) | async-done | bytes 65568 | tf_op jit(solution)/shard_map/all_to_all | solution.py:150
  67.5 3.5 %all-to-all-start.2 = ((f32[4,1,4096]{2,1,0:T(1,128)}), f32[4,1,4096]{2,1,0:T(1,128)S(1)}, u32[]{:S(2)}, u32[]{:S(2)}) async-start(f32[4,1,4096]{2,1,0:T(1,128)} %reshape.76), calls=%async_computation.2 | async-start | bytes 131072 | tf_op jit(solution)/shard_map/all_to_all | solution.py:151
  73.5 1.9 %all-to-all-done.2 = f32[4,1,4096]{2,1,0:T(1,128)S(1)} async-done(((f32[4,1,4096]{2,1,0:T(1,128)}), f32[4,1,4096]{2,1,0:T(1,128)S(1)}, u32[]{:S(2)}, u32[]{:S(2)}) %all-to-all-start.2) | async-done | bytes 65568 | tf_op jit(solution)/shard_map/all_to_all | solution.py:151
  78.8 16.9 %collective-permute-start.17 = (f32[2,16,16,32]{3,2,1,0:T(8,128)S(1)}, f32[2,16,16,32]{3,2,1,0:T(8,128)S(1)}, u32[]{:S(2)}, u32[]{:S(2)}) collective-permute-start(f32[2,16,16,32]{3,2,1,0:T(8,128)S(1)} %fusion.6), channel_id=1, source_target_pairs={{16,0},{17,1},{18,2},{19,3},{20,4},{21,5},{22,6},{23,7},{24,8},{25... | collective-permute-start | bytes 196616 | tf_op jit(solution)/shard_map/ppermute | solution.py:32
  (79 shorter events, 25.8 us)
Async XLA Ops:
  0.6 17.4 %collective-permute-start.4 = (f32[3,16,8,128]{3,2,1,0:T(8,128)}, f32[3,16,8,128]{3,2,1,0:T(8,128)S(1)}, u32[]{:S(2)}, u32[]{:S(2)}) collective-permute-start(f32[3,16,8,128]{3,2,1,0:T(8,128)} %bitcast.99), channel_id=1, source_target_pairs={{0,16},{1,17},{2,18},{3,19},{4,20},{5,21},{6,22},{7,23},{8,24},{9,... | collective-permute-start | bytes 589832 | tf_op jit(solution)/shard_map/ppermute | solution.py:32
  2.7 4.6 %collective-permute-start = (f32[3,1,8,128]{3,2,1,0:T(8,128)S(1)}, f32[3,1,8,128]{3,2,1,0:T(8,128)S(1)}, u32[]{:S(2)}, u32[]{:S(2)}) collective-permute-start(f32[3,1,8,128]{3,2,1,0:T(8,128)S(1)} %get-tuple-element.35), channel_id=1, source_target_pairs={{4,0},{8,4},{12,8},{0,12},{5,1},{9,5},{13,9},{1,13},{6,2},{10,6},{... | collective-permute-start | bytes 36872 | tf_op jit(solution)/shard_map/ppermute | solution.py:24
  5.7 3.4 %copy-start = (f32[1,3,16,8,128]{4,3,2,1,0:T(8,128)S(1)}, f32[1,3,16,8,128]{4,3,2,1,0:T(8,128)}, u32[]{:S(2)}) copy-start(f32[1,3,16,8,128]{4,3,2,1,0:T(8,128)} %param.2) | copy-start | bytes 589828
  5.7 3.4 %collective-permute-start.1 = (f32[3,1,8,128]{3,2,1,0:T(8,128)S(1)}, f32[3,1,8,128]{3,2,1,0:T(8,128)S(1)}, u32[]{:S(2)}, u32[]{:S(2)}) collective-permute-start(f32[3,1,8,128]{3,2,1,0:T(8,128)S(1)} %get-tuple-element.34), channel_id=1, source_target_pairs={{0,4},{4,8},{8,12},{12,0},{1,5},{5,9},{9,13},{13,1},{2,6},{6,10},{... | collective-permute-start | bytes 36872 | tf_op jit(solution)/shard_map/ppermute | solution.py:21
  9.1 4.4 %collective-permute-start.2 = (f32[3,18,1,128]{3,2,1,0:T(1,128)S(1)}, f32[3,18,1,128]{3,2,1,0:T(1,128)S(1)}, u32[]{:S(2)}, u32[]{:S(2)}) collective-permute-start(f32[3,18,1,128]{3,2,1,0:T(1,128)S(1)} %get-tuple-element.18), channel_id=1, source_target_pairs={{1,0},{2,1},{3,2},{0,3},{5,4},{6,5},{7,6},{4,7},{9,8},{10,9},{11,1... | collective-permute-start | bytes 82952 | tf_op jit(solution)/shard_map/ppermute | solution.py:24
  12.5 4.7 %collective-permute-start.3 = (f32[3,18,1,128]{3,2,1,0:T(1,128)S(1)}, f32[3,18,1,128]{3,2,1,0:T(1,128)S(1)}, u32[]{:S(2)}, u32[]{:S(2)}) collective-permute-start(f32[3,18,1,128]{3,2,1,0:T(1,128)S(1)} %get-tuple-element.17), channel_id=1, source_target_pairs={{0,1},{1,2},{2,3},{3,0},{4,5},{5,6},{6,7},{7,4},{8,9},{9,10},{10,1... | collective-permute-start | bytes 82952 | tf_op jit(solution)/shard_map/ppermute | solution.py:21
  18.4 2.6 %collective-permute-start.5 = (f32[3,1,8,128]{3,2,1,0:T(8,128)S(1)}, f32[3,1,8,128]{3,2,1,0:T(8,128)S(1)}, u32[]{:S(2)}, u32[]{:S(2)}) collective-permute-start(f32[3,1,8,128]{3,2,1,0:T(8,128)S(1)} %get-tuple-element.30), channel_id=1, source_target_pairs={{4,0},{8,4},{12,8},{0,12},{5,1},{9,5},{13,9},{1,13},{6,2},{10,6},{... | collective-permute-start | bytes 36872 | tf_op jit(solution)/shard_map/ppermute | solution.py:24
  18.7 3.4 %collective-permute-start.6 = (f32[3,1,8,128]{3,2,1,0:T(8,128)S(1)}, f32[3,1,8,128]{3,2,1,0:T(8,128)S(1)}, u32[]{:S(2)}, u32[]{:S(2)}) collective-permute-start(f32[3,1,8,128]{3,2,1,0:T(8,128)S(1)} %get-tuple-element.29), channel_id=1, source_target_pairs={{0,4},{4,8},{8,12},{12,0},{1,5},{5,9},{9,13},{13,1},{2,6},{6,10},{... | collective-permute-start | bytes 36872 | tf_op jit(solution)/shard_map/ppermute | solution.py:21
  22.2 2.8 %collective-permute-start.7 = (f32[3,18,1,128]{3,2,1,0:T(1,128)S(1)}, f32[3,18,1,128]{3,2,1,0:T(1,128)S(1)}, u32[]{:S(2)}, u32[]{:S(2)}) collective-permute-start(f32[3,18,1,128]{3,2,1,0:T(1,128)S(1)} %get-tuple-element.14), channel_id=1, source_target_pairs={{1,0},{2,1},{3,2},{0,3},{5,4},{6,5},{7,6},{4,7},{9,8},{10,9},{11,1... | collective-permute-start | bytes 82952 | tf_op jit(solution)/shard_map/ppermute | solution.py:24
  22.3 4.6 %collective-permute-start.8 = (f32[3,18,1,128]{3,2,1,0:T(1,128)S(1)}, f32[3,18,1,128]{3,2,1,0:T(1,128)S(1)}, u32[]{:S(2)}, u32[]{:S(2)}) collective-permute-start(f32[3,18,1,128]{3,2,1,0:T(1,128)S(1)} %get-tuple-element.13), channel_id=1, source_target_pairs={{0,1},{1,2},{2,3},{3,0},{4,5},{5,6},{6,7},{7,4},{8,9},{9,10},{10,1... | collective-permute-start | bytes 82952 | tf_op jit(solution)/shard_map/ppermute | solution.py:21
  28.0 3.5 %collective-permute-start.10 = (f32[3,1,8,128]{3,2,1,0:T(8,128)S(1)}, f32[3,1,8,128]{3,2,1,0:T(8,128)S(1)}, u32[]{:S(2)}, u32[]{:S(2)}) collective-permute-start(f32[3,1,8,128]{3,2,1,0:T(8,128)S(1)} %get-tuple-element.24), channel_id=1, source_target_pairs={{0,4},{4,8},{8,12},{12,0},{1,5},{5,9},{9,13},{13,1},{2,6},{6,10},{... | collective-permute-start | bytes 36872 | tf_op jit(solution)/shard_map/ppermute | solution.py:21
  28.3 3.2 %collective-permute-start.9 = (f32[3,1,8,128]{3,2,1,0:T(8,128)S(1)}, f32[3,1,8,128]{3,2,1,0:T(8,128)S(1)}, u32[]{:S(2)}, u32[]{:S(2)}) collective-permute-start(f32[3,1,8,128]{3,2,1,0:T(8,128)S(1)} %get-tuple-element.25), channel_id=1, source_target_pairs={{4,0},{8,4},{12,8},{0,12},{5,1},{9,5},{13,9},{1,13},{6,2},{10,6},{... | collective-permute-start | bytes 36872 | tf_op jit(solution)/shard_map/ppermute | solution.py:24
  31.5 2.8 %collective-permute-start.11 = (f32[3,18,1,128]{3,2,1,0:T(1,128)S(1)}, f32[3,18,1,128]{3,2,1,0:T(1,128)S(1)}, u32[]{:S(2)}, u32[]{:S(2)}) collective-permute-start(f32[3,18,1,128]{3,2,1,0:T(1,128)S(1)} %get-tuple-element.10), channel_id=1, source_target_pairs={{1,0},{2,1},{3,2},{0,3},{5,4},{6,5},{7,6},{4,7},{9,8},{10,9},{11,1... | collective-permute-start | bytes 82952 | tf_op jit(solution)/shard_map/ppermute | solution.py:24
  31.8 4.5 %collective-permute-start.12 = (f32[3,18,1,128]{3,2,1,0:T(1,128)S(1)}, f32[3,18,1,128]{3,2,1,0:T(1,128)S(1)}, u32[]{:S(2)}, u32[]{:S(2)}) collective-permute-start(f32[3,18,1,128]{3,2,1,0:T(1,128)S(1)} %get-tuple-element.9), channel_id=1, source_target_pairs={{0,1},{1,2},{2,3},{3,0},{4,5},{5,6},{6,7},{7,4},{8,9},{9,10},{10,1... | collective-permute-start | bytes 82952 | tf_op jit(solution)/shard_map/ppermute | solution.py:21
  37.5 8.7 %copy-start.1 = (f32[3,16,8,128]{3,2,1,0:T(8,128)}, f32[3,16,8,128]{3,2,1,0:T(8,128)S(1)}, u32[]{:S(2)}) copy-start(f32[3,16,8,128]{3,2,1,0:T(8,128)S(1)} %multiply_add_fusion) | copy-start | bytes 589828
  37.5 3.5 %collective-permute-start.13 = (f32[3,1,8,128]{3,2,1,0:T(8,128)S(1)}, f32[3,1,8,128]{3,2,1,0:T(8,128)S(1)}, u32[]{:S(2)}, u32[]{:S(2)}) collective-permute-start(f32[3,1,8,128]{3,2,1,0:T(8,128)S(1)} %get-tuple-element.19), channel_id=1, source_target_pairs={{0,4},{4,8},{8,12},{12,0},{1,5},{5,9},{9,13},{13,1},{2,6},{6,10},{... | collective-permute-start | bytes 36872 | tf_op jit(solution)/shard_map/ppermute | solution.py:21
  38.9 2.5 %collective-permute-start.14 = (f32[3,1,8,128]{3,2,1,0:T(8,128)S(1)}, f32[3,1,8,128]{3,2,1,0:T(8,128)S(1)}, u32[]{:S(2)}, u32[]{:S(2)}) collective-permute-start(f32[3,1,8,128]{3,2,1,0:T(8,128)S(1)} %get-tuple-element.20), channel_id=1, source_target_pairs={{4,0},{8,4},{12,8},{0,12},{5,1},{9,5},{13,9},{1,13},{6,2},{10,6},{... | collective-permute-start | bytes 36872 | tf_op jit(solution)/shard_map/ppermute | solution.py:24
  41.5 4.6 %collective-permute-start.15 = (f32[3,18,1,128]{3,2,1,0:T(1,128)S(1)}, f32[3,18,1,128]{3,2,1,0:T(1,128)S(1)}, u32[]{:S(2)}, u32[]{:S(2)}) collective-permute-start(f32[3,18,1,128]{3,2,1,0:T(1,128)S(1)} %get-tuple-element.5), channel_id=1, source_target_pairs={{0,1},{1,2},{2,3},{3,0},{4,5},{5,6},{6,7},{7,4},{8,9},{9,10},{10,1... | collective-permute-start | bytes 82952 | tf_op jit(solution)/shard_map/ppermute | solution.py:21
  41.6 4.5 %collective-permute-start.16 = (f32[3,18,1,128]{3,2,1,0:T(1,128)S(1)}, f32[3,18,1,128]{3,2,1,0:T(1,128)S(1)}, u32[]{:S(2)}, u32[]{:S(2)}) collective-permute-start(f32[3,18,1,128]{3,2,1,0:T(1,128)S(1)} %get-tuple-element.6), channel_id=1, source_target_pairs={{1,0},{2,1},{3,2},{0,3},{5,4},{6,5},{7,6},{4,7},{9,8},{10,9},{11,1... | collective-permute-start | bytes 82952 | tf_op jit(solution)/shard_map/ppermute | solution.py:24
  58.4 9.1 %all-to-all-start.1 = ((f32[4,1,4096]{2,1,0:T(1,128)}), f32[4,1,4096]{2,1,0:T(1,128)S(1)}, u32[]{:S(2)}, u32[]{:S(2)}) async-start(f32[4,1,4096]{2,1,0:T(1,128)} %reshape.78), calls=%async_computation.1 | async-start | bytes 131072 | tf_op jit(solution)/shard_map/all_to_all | solution.py:150
  67.5 7.9 %all-to-all-start.2 = ((f32[4,1,4096]{2,1,0:T(1,128)}), f32[4,1,4096]{2,1,0:T(1,128)S(1)}, u32[]{:S(2)}, u32[]{:S(2)}) async-start(f32[4,1,4096]{2,1,0:T(1,128)} %reshape.76), calls=%async_computation.2 | async-start | bytes 131072 | tf_op jit(solution)/shard_map/all_to_all | solution.py:151
  78.8 18.0 %collective-permute-start.17 = (f32[2,16,16,32]{3,2,1,0:T(8,128)S(1)}, f32[2,16,16,32]{3,2,1,0:T(8,128)S(1)}, u32[]{:S(2)}, u32[]{:S(2)}) collective-permute-start(f32[2,16,16,32]{3,2,1,0:T(8,128)S(1)} %fusion.6), channel_id=1, source_target_pairs={{16,0},{17,1},{18,2},{19,3},{20,4},{21,5},{22,6},{23,7},{24,8},{25... | collective-permute-start | bytes 196616 | tf_op jit(solution)/shard_map/ppermute | solution.py:32
where the time goes:
time: 98.3 us; the launch traced here: 97.5 us
  starting transfers between devices  45.3 us (46%)
  waiting for transfers between devices  24.4 us (25%)
  local copies, waits for them, and re-layouts  9.25 us (9%)
  other arithmetic  7.8 us (8%)
  blocking collectives  6.68 us (7%)
  matrix products  2.52 us (3%)
  between operations  1.66 us (2%)
    ppermute x2, starting transfers between devices, from_behind(): return lax.ppermute(shard, axis, pairs)  18.2 us
    ppermute x8, waiting for transfers between devices, with_halo(): lax.ppermute(lax.slice_in_dim(block, block.shape[dim] - width, None, axis...  14.1 us
    ppermute x8, starting transfers between devices, with_halo(): lax.ppermute(lax.slice_in_dim(block, 0, width, axis=dim), axis, backward)  13.4 us
    all_to_all x1, blocking collectives, on_device(): lax.all_to_all(tile_block, 'gx', split_axis=3, concat_axis=0, tiled=True)  6.68 us
    ppermute x8, starting transfers between devices, with_halo(): lax.ppermute(lax.slice_in_dim(block, block.shape[dim] - width, None, axis...  5.63 us
    ppermute x8, waiting for transfers between devices, with_halo(): lax.ppermute(lax.slice_in_dim(block, 0, width, axis=dim), axis, backward)  4.9 us
    unnamed x10, local copies, waits for them, and re-layouts  4.58 us
    all_to_all x1, starting transfers between devices, on_device(): lax.all_to_all(real_part, 'gy', split_axis=3, concat_axis=0, tiled=True)  4.52 us
  transfers between devices with their start and end apart: 20, of which 16 were waited for; matrix products, arithmetic and copies ran while one was open for 7% of the time, Pallas kernels for 0%

commit v1 on v0

v1 whole, which is shorter than its diff:
```python
import functools
import math

import jax
import jax.numpy as jnp
import numpy as np
from jax import lax
from jax.experimental import pallas as pl
from jax.experimental.pallas import tpu as pltpu
from jax.sharding import PartitionSpec as P

time_step = 0.1
fringe_rate = 1.0
smag_coef = 0.03
base_visc = 0.02
strain_floor = 0.25
MESH = pl.DeviceIdType.MESH
WIDE = 4
BASE = 8


def from_behind(shard, axis, by):
    peers = lax.axis_size(axis)
    pairs = [(i, i + by) for i in range(peers) if 0 <= i + by < peers]
    return lax.ppermute(shard, axis, pairs)


def partner_half(values):
    return from_behind(values, "dom", -1)


def dft_tables(length):
    positions = jnp.arange(length, dtype=jnp.int32)
    phase = (positions[:, None] * positions[None, :] % length).astype(jnp.float32) * (
        2.0 * math.pi / length
    )
    factor = 1.0 / math.sqrt(length)
    return (jnp.cos(phase) * factor, jnp.sin(phase) * factor)


def step_kernel(sizes, fused, *refs):
    tiles_x, tiles_y, cells_x, cells_y, levels_z, fringe_len = sizes
    if fused:
        (fs_ref, u_hbm, tx_hbm, ty_hbm, v_hbm, spec_ref, *scratch) = refs
    else:
        (fs_ref, u_hbm, v_hbm, div_ref, *scratch) = refs
    (U, I, S1, S2, S3, edge, near, near_in, diag, diag_in, ramp) = scratch[:11]
    (load_sem, send_sem, recv_sem, in_send, in_recv, out_sem) = scratch[11:17]
    if fused:
        tx, ty, rows, block, got, turned, tab_sem, blk_send, blk_recv, own_sem = scratch[17:]
    dom, gx, gy = (lax.axis_index(name) for name in ("dom", "gx", "gy"))
    count = 2 * tiles_x * tiles_y
    me = (dom * tiles_x + gx) * tiles_y + gy
    total_x = cells_x * tiles_x
    hi = WIDE + cells_x
    inner = pl.ds(BASE, cells_y)

    def at(index):
        return (
            index // (tiles_x * tiles_y),
            lax.rem(index // tiles_y, tiles_x),
            lax.rem(index, tiles_y),
        )

    def beside(domain, dx, dy):
        return (
            domain,
            lax.rem(gx + dx + tiles_x, tiles_x),
            lax.rem(gy + dy + tiles_y, tiles_y),
        )

    around = [(1, 0), (-1, 0), (0, 1), (0, -1), (1, 1), (1, -1), (-1, 1), (-1, -1)]
    barrier = pltpu.get_barrier_semaphore()
    if fused:
        @pl.loop(1, count)
        def _(i):
            pl.semaphore_signal(
                barrier, inc=1, device_id=at(lax.rem(me + i, count)), device_id_type=MESH
            )
    else:
        for dx, dy in around:
            for domain in range(2):
                pl.semaphore_signal(
                    barrier, inc=1, device_id=beside(domain, dx, dy), device_id_type=MESH
                )
        pl.semaphore_signal(barrier, inc=1, device_id=beside(1 - dom, 0, 0), device_id_type=MESH)

    load = pltpu.make_async_copy(u_hbm.at[0], U.at[:, pl.ds(WIDE, cells_x), inner, :], load_sem)
    load.start()
    if fused:
        tab_x = pltpu.make_async_copy(tx_hbm.at[gy], tx, tab_sem.at[0])
        tab_y = pltpu.make_async_copy(ty_hbm, ty, tab_sem.at[1])
        tab_x.start()
        tab_y.start()

    cell = lax.broadcasted_iota(jnp.int32, ramp.shape, 0) + (gx * cells_x - WIDE)
    offset = cell - fs_ref[0]
    for _ in range(2):
        offset = jnp.where(offset < 0, offset + total_x, offset)
    offset = jnp.where(offset >= total_x, offset - total_x, offset)
    sine = jnp.sin((offset.astype(jnp.float32) + 0.5) * (math.pi / fringe_len))
    farm = dom.astype(jnp.float32)
    ramp[...] = jnp.where(offset < fringe_len, fringe_rate * sine * sine, 0.0) * farm

    @pl.when(dom == 0)
    def _():
        I[...] = jnp.zeros_like(I)

    load.wait()
    edge[0] = U[:, WIDE:hi, BASE : BASE + WIDE, :]
    edge[1] = U[:, WIDE:hi, BASE + cells_y - WIDE : BASE + cells_y, :]
    pl.semaphore_wait(barrier, count - 1 if fused else 17)

    def margins(domain, field, strips, corners, sends, recvs):
        low, high = pl.ds(0, WIDE), pl.ds(hi, WIDE)
        pieces = []
        for dx, dy in around:
            mine = pl.ds(cells_x, WIDE) if dx > 0 else pl.ds(WIDE, WIDE)
            if dy == 0:
                pieces.append((U.at[:, mine, inner, :], field.at[:, low if dx > 0 else high, inner, :]))
            elif dx == 0:
                pieces.append((edge.at[1 if dy > 0 else 0], strips.at[0 if dy > 0 else 1]))
            else:
                part = pl.ds(cells_x - WIDE if dx > 0 else 0, WIDE)
                pieces.append((
                    edge.at[1 if dy > 0 else 0, :, part],
                    corners.at[0 if dx > 0 else 1, 0 if dy > 0 else 1],
                ))
        return [
            pltpu.make_async_remote_copy(
                src_ref=source, dst_ref=target, send_sem=sends.at[i], recv_sem=recvs.at[i],
                device_id=beside(domain, *around[i]), device_id_type=MESH,
            )
            for i, (source, target) in enumerate(pieces)
        ]

    def place(field, strips, corners):
        for side in range(2):
            span = pl.ds(BASE - WIDE if side == 0 else BASE + cells_y, WIDE)
            field[:, WIDE:hi, span, :] = strips[side]
            field[:, 0:WIDE, span, :] = corners[0, side]
            field[:, hi : hi + WIDE, span, :] = corners[1, side]

    own = margins(dom, U, near, diag, send_sem, recv_sem)
    inflow = margins(1, I, near_in, diag_in, in_send, in_recv)
    block_in = pltpu.make_async_remote_copy(
        src_ref=U.at[:, pl.ds(WIDE, cells_x), inner, :],
        dst_ref=I.at[:, pl.ds(WIDE, cells_x), inner, :],
        send_sem=in_send.at[8], recv_sem=in_recv.at[8],
        device_id=(1 - dom, gx, gy), device_id_type=MESH,
    )
    order = [4, 5, 6, 7, 2, 3, 0, 1]
    for i in order:
        own[i].start()

    @pl.when(dom == 0)
    def _():
        for i in order:
            inflow[i].start()
        block_in.start()

    for copy in own:
        copy.wait_recv()
    place(U, near, diag)

    @pl.when(dom == 1)
    def _():
        for copy in inflow:
            copy.wait_recv()
        block_in.wait_recv()
        place(I, near_in, diag_in)

    lane = lax.broadcasted_iota(jnp.int32, (8, levels_z), 1)
    first, last = lane == 0, lane == levels_z - 1

    def rate(field, x, row):
        centre = [field[c, x, pl.ds(row, 8), :] for c in range(3)]
        grads, laps = [[], [], []], []
        for c in range(3):
            xp, xm = field[c, x + 1, pl.ds(row, 8), :], field[c, x - 1, pl.ds(row, 8), :]
            yp, ym = field[c, x, pl.ds(row + 1, 8), :], field[c, x, pl.ds(row - 1, 8), :]
            zp = jnp.where(last, 0.0, pltpu.roll(centre[c], levels_z - 1, 1))
            zm = jnp.where(first, 0.0, pltpu.roll(centre[c], 1, 1))
            grads[0].append(xp - xm)
            grads[1].append(yp - ym)
            grads[2].append(zp - zm)
            laps.append((xp + xm) + (yp + ym) + (zp + zm) - 6.0 * centre[c])
        (axx, axy, axz), (ayx, ayy, ayz), (azx, azy, azz) = grads
        shear = (axy + ayx, axz + azx, ayz + azy)
        diagonal = axx * axx + ayy * ayy + azz * azz
        sheared = shear[0] * shear[0] + shear[1] * shear[1] + shear[2] * shear[2]
        under = 0.5 * diagonal + (0.25 * sheared + strain_floor)
        eddy = base_visc + smag_coef * (under * lax.rsqrt(under))
        pull = jnp.broadcast_to(ramp[pl.ds(x, 1), :], (8, levels_z))
        rates = []
        for c in range(3):
            carried = centre[0] * grads[0][c] + centre[1] * grads[1][c] + centre[2] * grads[2][c]
            behind = I[c, x, pl.ds(row, 8), :] - centre[c]
            rates.append(eddy * laps[c] - 0.5 * carried + pull * behind)
        return centre, rates

    def stage(field, result, margin, finish):
        starts = (BASE - margin, BASE + cells_y + margin - 8)

        @pl.loop(WIDE - margin, hi + margin)
        def _(x):
            for row in starts:
                centre, rates = rate(field, x, row)
                for c in range(3):
                    result[c, x, pl.ds(row, 8), :] = finish(
                        U[c, x, pl.ds(row, 8), :], centre[c] + time_step * rates[c]
                    )

    stage(U, S1, 3, lambda start, moved: moved)
    stage(S1, S2, 2, lambda start, moved: 0.75 * start + 0.25 * moved)
    stage(S2, S3, 1, lambda start, moved: (1.0 / 3.0) * start + (2.0 / 3.0) * moved)

    out = pltpu.make_async_copy(S3.at[:, pl.ds(WIDE, cells_x), inner, :], v_hbm.at[0], out_sem)
    out.start()

    def divergence(x):
        w = S3[2, x, inner, :]
        up = jnp.where(last, 0.0, pltpu.roll(w, levels_z - 1, 1))
        down = jnp.where(first, 0.0, pltpu.roll(w, 1, 1))
        along = 0.5 * (S3[0, x + 1, inner, :] - S3[0, x - 1, inner, :])
        across = 0.5 * (S3[1, x, pl.ds(BASE + 1, 8), :] - S3[1, x, pl.ds(BASE - 1, 8), :])
        return along + across + 0.5 * (up - down)

    if not fused:
        for x in range(cells_x):
            div_ref[x] = divergence(x + WIDE)
    else:
        parts = 2 * tiles_x
        depth = levels_z // parts
        group = lax.broadcasted_iota(jnp.int32, (cells_x, levels_z), 1) // depth

        def block_copy(i):
            target = lax.rem(me + i, count)
            return pltpu.make_async_remote_copy(
                src_ref=block.at[target // tiles_y], dst_ref=got.at[gy, gx],
                send_sem=blk_send.at[i], recv_sem=blk_recv,
                device_id=at(target), device_id_type=MESH,
            )

        @pl.when(dom == 1)
        def _():
            for x in range(cells_x):
                rows[x * cells_y : (x + 1) * cells_y, :] = divergence(x + WIDE)
            pieces = [None] * parts
            for y in range(cells_y):
                line = rows[pl.ds(y, cells_x, stride=cells_y), :]
                for p in range(parts):
                    by = ((y - p) * depth) % levels_z
                    moved = pltpu.roll(line, by, 1) if by else line
                    pieces[p] = moved if y == 0 else jnp.where(group == y, moved, pieces[p])
            for p in range(parts):
                block[p] = pieces[p]
            for i in range(1, count):
                block_copy(i).start()
            pltpu.make_async_copy(block.at[me // tiles_y], got.at[gy, gx], blk_recv).start()

        tab_x.wait()
        tab_y.wait()
        pltpu.make_async_copy(got, got, blk_recv).wait()
        highest = lax.Precision.HIGHEST
        for g in range(tiles_y):
            lines = got[g].reshape(total_x, levels_z)
            partly = jnp.dot(tx[...], lines, precision=highest, preferred_element_type=jnp.float32)
            turned[g * levels_z : (g + 1) * levels_z, :] = partly.T
        total_y = cells_y * tiles_y
        waves = total_x // tiles_y
        wide = 2 * waves
        each = levels_z // wide
        chunk = lax.broadcasted_iota(jnp.int32, (total_y, levels_z), 1) // wide
        for q in range(depth // each):
            packed = None
            for j in range(each):
                level = turned[pl.ds(q * each + j, total_y, stride=depth), :]
                packed = level if j == 0 else jnp.where(chunk == j, level, packed)
            both = jnp.dot(packed.T, ty[...], precision=highest, preferred_element_type=jnp.float32)
            for j in range(each):
                real = both[j * wide : j * wide + waves]
                imag = both[j * wide + waves : (j + 1) * wide]
                whole = real + pltpu.roll(imag, 2 * total_y, 1)
                spec_ref[0, q * each + j] = whole[:, :total_y]
                spec_ref[1, q * each + j] = whole[:, total_y : 2 * total_y]

        @pl.when(dom == 1)
        def _():
            for i in range(1, count):
                block_copy(i).wait_send()

    for copy in own:
        copy.wait_send()

    @pl.when(dom == 0)
    def _():
        for copy in inflow:
            copy.wait_send()
        block_in.wait_send()

    out.wait()


def tables(tiles_y, total_x, total_y, each):
    waves = total_x // tiles_y
    turn = 2.0 * np.pi / total_x * (np.outer(np.arange(total_x), np.arange(total_x)) % total_x)
    cosine, sine = np.cos(turn) / np.sqrt(total_x), -np.sin(turn) / np.sqrt(total_x)
    along = np.stack([cosine.reshape(tiles_y, waves, total_x), sine.reshape(tiles_y, waves, total_x)], 1)
    along = np.tile(along.reshape(tiles_y, 2 * waves, total_x), (1, each, 1))
    turn = 2.0 * np.pi / total_y * (np.outer(np.arange(total_y), np.arange(total_y)) % total_y)
    cosine, sine = np.cos(turn) / np.sqrt(total_y), np.sin(turn) / np.sqrt(total_y)
    across = np.concatenate([cosine, -sine, sine, cosine], 1)
    return along.astype(np.float32), across.astype(np.float32)


def on_device(tiles_x, tiles_y, velocity, fringe_start):
    _, _, cells_x, cells_y, levels_z = velocity.shape
    total_x, total_y = cells_x * tiles_x, cells_y * tiles_y
    fringe_len = min(8 * cells_x, total_x // 2)
    parts = 2 * tiles_x
    depth = levels_z // parts
    waves = total_x // tiles_y
    fused = cells_y * depth == levels_z and 4 * total_y == levels_z and 8 * waves == levels_z
    sizes = (tiles_x, tiles_y, cells_x, cells_y, levels_z, fringe_len)
    field = pltpu.VMEM((3, cells_x + 2 * WIDE, cells_y + 2 * BASE, levels_z), jnp.float32)
    strips = pltpu.VMEM((2, 3, cells_x, WIDE, levels_z), jnp.float32)
    corners = pltpu.VMEM((2, 2, 3, WIDE, WIDE, levels_z), jnp.float32)
    dma = pltpu.SemaphoreType.DMA
    scratch = [field] * 5 + [strips] * 3 + [corners] * 2
    scratch += [pltpu.VMEM((cells_x + 2 * WIDE, levels_z), jnp.float32)]
    scratch += [dma, dma((8,)), dma((8,)), dma((9,)), dma((9,)), dma]
    anywhere, vmem = pl.BlockSpec(memory_space=pl.ANY), pl.BlockSpec(memory_space=pltpu.VMEM)
    args = [fringe_start, velocity]
    in_specs = [pl.BlockSpec(memory_space=pltpu.SMEM), anywhere]
    if fused:
        along, across = tables(tiles_y, total_x, total_y, levels_z // (2 * waves))
        args += [jnp.asarray(along), jnp.asarray(across)]
        in_specs += [anywhere, anywhere]
        second = (2, depth, waves, total_y)
        scratch += [
            pltpu.VMEM(along.shape[1:], jnp.float32),
            pltpu.VMEM(across.shape, jnp.float32),
            pltpu.VMEM((cells_x * cells_y, levels_z), jnp.float32),
            pltpu.VMEM((parts, cells_x, levels_z), jnp.float32),
            pltpu.VMEM((tiles_y, tiles_x, cells_x, levels_z), jnp.float32),
            pltpu.VMEM((tiles_y * levels_z, levels_z), jnp.float32),
            dma((2,)), dma((parts * tiles_y,)), dma, dma,
        ]
    else:
        second = (cells_x, cells_y, levels_z)
    field_out, other = pl.pallas_call(
        functools.partial(step_kernel, sizes, fused),
        out_shape=(
            jax.ShapeDtypeStruct(velocity.shape, jnp.float32),
            jax.ShapeDtypeStruct(second, jnp.float32),
        ),
        in_specs=in_specs,
        out_specs=(anywhere, vmem),
        scratch_shapes=scratch,
        compiler_params=pltpu.CompilerParams(
            collective_id=0, has_side_effects=True, vmem_limit_bytes=32 * 1024 * 1024
        ),
        name="farm_step",
    )(*args)
    if fused:
        return field_out, other
    return field_out, spectrum_of(other)


def spectrum_of(divergence):
    cells_x, cells_y, levels_z = divergence.shape
    tiles_x = lax.axis_size("gx")
    total_x, total_y = cells_x * tiles_x, cells_y * lax.axis_size("gy")
    is_farm = lax.axis_index("dom") == 1
    levels_out = levels_z // (2 * tiles_x)
    tile_block = divergence.reshape(cells_x, cells_y, 2, tiles_x, levels_out)
    highest = lax.Precision.HIGHEST
    cos_table_x, sin_table_x = dft_tables(total_x)
    cos_table_y, sin_table_y = dft_tables(total_y)
    shard_piece = lax.all_to_all(tile_block, "gx", split_axis=3, concat_axis=0, tiled=True)
    real_part = jnp.einsum("xyhgc,xk->yhck", shard_piece, cos_table_x, precision=highest)
    imag_part = -jnp.einsum("xyhgc,xk->yhck", shard_piece, sin_table_x, precision=highest)
    real_part, imag_part = (real_part, imag_part)
    real_in = lax.all_to_all(real_part, "gy", split_axis=3, concat_axis=0, tiled=True)
    imag_in = lax.all_to_all(imag_part, "gy", split_axis=3, concat_axis=0, tiled=True)
    real_out = jnp.einsum("yhck,yj->hckj", real_in, cos_table_y, precision=highest) + jnp.einsum(
        "yhck,yj->hckj", imag_in, sin_table_y, precision=highest
    )
    imag_out = jnp.einsum("yhck,yj->hckj", imag_in, cos_table_y, precision=highest) - jnp.einsum(
        "yhck,yj->hckj", real_in, sin_table_y, precision=highest
    )
    packed = jnp.stack([real_out, imag_out])
    received = partner_half(packed[:, 0])
    spectrum = jnp.where(is_farm, packed[:, 1], received)
    return spectrum


def solution(mesh):
    in_specs = (P("dom", None, "gx", "gy", None), P())
    out_specs = (P("dom", None, "gx", "gy", None), P(None, ("dom", "gx"), "gy", None))
    return jax.shard_map(
        functools.partial(on_device, mesh.shape["gx"], mesh.shape["gy"]),
        mesh=mesh, in_specs=in_specs, out_specs=out_specs, check_vma=False,
    )
```

time: 98.3 us -> 37 us (0.38)
  starting transfers between devices: 45.3 us -> 0 us
  Pallas kernels: 0 us -> 31.5 us
  waiting for transfers between devices: 24.4 us -> 0 us
  other arithmetic: 7.8 us -> 0 us
  blocking collectives: 6.68 us -> 0 us
  local copies, waits for them, and re-layouts: 9.25 us -> 3.97 us
  matrix products: 2.52 us -> 0 us
    ppermute x18 -> x0, starting transfers between devices: 37.3 us -> none  [the longest x2 18.2 us: from_behind(): return lax.ppermute(shard, axis, pairs)]
    pallas_call x0 -> x1, Pallas kernels: none -> 31.5 us  [on_device(): pl.pallas_call(functools.partial(step_kernel, sizes, fused), out_shape=(j...]
    ppermute x18 -> x0, waiting for transfers between devices: 20.1 us -> none  [the longest x8 14.1 us: with_halo(): lax.ppermute(lax.slice_in_dim(block, block.shape[dim] - width, None, axis...]
    all_to_all x2 -> x0, starting transfers between devices: 7.99 us -> none  [the longest x1 4.52 us: on_device(): lax.all_to_all(real_part, 'gy', split_axis=3, concat_axis=0, tiled=True)]
    all_to_all x1 -> x0, blocking collectives: 6.68 us -> none  [on_device(): lax.all_to_all(tile_block, 'gx', split_axis=3, concat_axis=0, tiled=True)]
    all_to_all x2 -> x0, waiting for transfers between devices: 4.27 us -> none  [the longest x1 2.4 us: on_device(): lax.all_to_all(real_part, 'gy', split_axis=3, concat_axis=0, tiled=True)]
    dot_general x6 -> x0, matrix products: 2.52 us -> none  [the longest x1 0.44 us: on_device(): jnp.einsum('yhck,yj->hckj', real_in, cos_table_y, precision=highest)]
    all_to_all x3 -> x0, other arithmetic: 2.32 us -> none  [the longest x1 0.77 us: on_device(): lax.all_to_all(real_part, 'gy', split_axis=3, concat_axis=0, tiled=True)]
  transfers between devices with their start and end apart: 20 -> 0, of which waited for: 16 -> 0; matrix products, arithmetic and copies ran while one was open for 7% -> 0% of each run, Pallas kernels for 0% -> 0%
where the time goes in v1:
time: 37 us; the launch traced here: 36.7 us
  Pallas kernels  31.5 us (85%)
  local copies, waits for them, and re-layouts  3.97 us (11%)
  between operations  1.29 us (3%)
    pallas_call x1, Pallas kernels, on_device(): pl.pallas_call(functools.partial(step_kernel, sizes, fused), out_shape=(j...  31.5 us
    unnamed x8, local copies, waits for them, and re-layouts  3.97 us

profile of v1, /device:TPU:1, one launch (start us, length us, event | category | flops | bytes accessed | tf_op | source)
XLA Modules:
  0.0 36.7 jit_solution(548987631715396749)
XLA Ops:
  1.3 0.0 copy-start
  1.3 0.9 %copy-done = f32[4,128,64]{2,1,0:T(8,128)S(1)} copy-done((f32[4,128,64]{2,1,0:T(8,128)S(1)}, f32[4,128,64]{2,1,0:T(8,128)}, u32[]{:S(2)}) %copy-start) | copy-done | bytes 131096
  2.2 0.0 copy-start.1
  2.2 0.9 %copy-done.1 = f32[1,3,16,8,128]{4,3,2,1,0:T(8,128)S(1)} copy-done((f32[1,3,16,8,128]{4,3,2,1,0:T(8,128)S(1)}, f32[1,3,16,8,128]{4,3,2,1,0:T(8,128)}, u32[]{:S(2)}) %copy-start.1) | copy-done | bytes 196632
  3.2 0.0 copy-start.2
  3.2 0.7 %copy-done.2 = f32[32,128]{1,0:T(8,128)S(1)} copy-done((f32[32,128]{1,0:T(8,128)S(1)}, f32[32,128]{1,0:T(8,128)}, u32[]{:S(2)}) %copy-start.2) | copy-done | bytes 16408
  3.9 31.5 %farm_step.1 = (f32[1,3,16,8,128]{4,3,2,1,0:T(8,128)S(1)}, f32[2,16,16,32]{3,2,1,0:T(8,128)S(1)}) custom-call(s32[1]{0:T(128)S(6)} %copy.8.refs_0_, f32[1,3,16,8,128]{4,3,2,1,0:T(8,128)S(1)} %copy-done.1, f32[4,128,64]{2,1,0:T(8,128)S(1)} %copy-done, f32[32,128]{1,0:T(8,128)S(1)} %copy-done.2), custom_call_target="tpu_custom_call" | custom-call | tf_op jit(solution)/shard_map/farm_step/pallas_call | solution.py:352
  35.4 0.7 %copy.9 = f32[1,3,16,8,128]{4,3,2,1,0:T(8,128)} copy(f32[1,3,16,8,128]{4,3,2,1,0:T(8,128)S(1)} %get-tuple-element.4) | data formatting | bytes 393216
  36.0 0.7 %copy.10 = f32[2,16,16,32]{3,2,1,0:T(8,128)} copy(f32[2,16,16,32]{3,2,1,0:T(8,128)S(1)} %get-tuple-element.5) | data formatting | bytes 131072
Async XLA Ops:
  1.3 1.0 %copy-start = (f32[4,128,64]{2,1,0:T(8,128)S(1)}, f32[4,128,64]{2,1,0:T(8,128)}, u32[]{:S(2)}) copy-start(f32[4,128,64]{2,1,0:T(8,128)} %constant.4.clone.refs_2_) | copy-start | bytes 393220
  2.2 0.9 %copy-start.1 = (f32[1,3,16,8,128]{4,3,2,1,0:T(8,128)S(1)}, f32[1,3,16,8,128]{4,3,2,1,0:T(8,128)}, u32[]{:S(2)}) copy-start(f32[1,3,16,8,128]{4,3,2,1,0:T(8,128)} %refs_1_.1) | copy-start | bytes 589828
  3.2 0.7 %copy-start.2 = (f32[32,128]{1,0:T(8,128)S(1)}, f32[32,128]{1,0:T(8,128)}, u32[]{:S(2)}) copy-start(f32[32,128]{1,0:T(8,128)} %constant.5.clone.refs_3_) | copy-start | bytes 49156

commit v2 on v1

--- a/solution.py
+++ b/solution.py
@@ -44,10 +44,10 @@
         (fs_ref, u_hbm, tx_hbm, ty_hbm, v_hbm, spec_ref, *scratch) = refs
     else:
         (fs_ref, u_hbm, v_hbm, div_ref, *scratch) = refs
-    (U, I, S1, S2, S3, edge, near, near_in, diag, diag_in, ramp) = scratch[:11]
-    (load_sem, send_sem, recv_sem, in_send, in_recv, out_sem) = scratch[11:17]
-    if fused:
-        tx, ty, rows, block, got, turned, tab_sem, blk_send, blk_recv, own_sem = scratch[17:]
+    (U, I, S1, S2, S3, edge, near, near_in, tips, diag, diag_in, ramp) = scratch[:12]
+    (load_sem, send_sem, recv_sem, in_send, in_recv, out_sem) = scratch[12:18]
+    if fused:
+        tx, ty, rows, block, got, turned, tab_sem, blk_send, blk_recv = scratch[18:]
     dom, gx, gy = (lax.axis_index(name) for name in ("dom", "gx", "gy"))
     count = 2 * tiles_x * tiles_y
     me = (dom * tiles_x + gx) * tiles_y + gy
@@ -107,24 +107,32 @@
         I[...] = jnp.zeros_like(I)
 
     load.wait()
-    edge[0] = U[:, WIDE:hi, BASE : BASE + WIDE, :]
-    edge[1] = U[:, WIDE:hi, BASE + cells_y - WIDE : BASE + cells_y, :]
+    for side in range(2):
+        start = BASE if side == 0 else BASE + cells_y - WIDE
+        for c in range(3):
+            for j in range(WIDE):
+                edge[side, c, j] = U[c, WIDE:hi, start + j, :]
+        tips[0, side] = U[:, hi - WIDE : hi, start : start + WIDE, :]
+        tips[1, side] = U[:, WIDE : 2 * WIDE, start : start + WIDE, :]
     pl.semaphore_wait(barrier, count - 1 if fused else 17)
 
-    def margins(domain, field, strips, corners, sends, recvs):
-        low, high = pl.ds(0, WIDE), pl.ds(hi, WIDE)
+    def margins(domain, field, strips, corners, sends, recvs, width):
+        low, high = pl.ds(WIDE - width, width), pl.ds(hi, width)
+        less = width - 1
         pieces = []
         for dx, dy in around:
-            mine = pl.ds(cells_x, WIDE) if dx > 0 else pl.ds(WIDE, WIDE)
+            mine = pl.ds(hi - width, width) if dx > 0 else pl.ds(WIDE, width)
+            side = 1 if dy > 0 else 0
+            span = pl.ds(WIDE - width if dy > 0 else 0, width)
             if dy == 0:
                 pieces.append((U.at[:, mine, inner, :], field.at[:, low if dx > 0 else high, inner, :]))
             elif dx == 0:
-                pieces.append((edge.at[1 if dy > 0 else 0], strips.at[0 if dy > 0 else 1]))
+                pieces.append((edge.at[side, :, span], strips.at[1 - side, :, span]))
             else:
-                part = pl.ds(cells_x - WIDE if dx > 0 else 0, WIDE)
+                part = pl.ds(WIDE - less if dx > 0 else 0, less)
                 pieces.append((
-                    edge.at[1 if dy > 0 else 0, :, part],
-                    corners.at[0 if dx > 0 else 1, 0 if dy > 0 else 1],
+                    tips.at[0 if dx > 0 else 1, side, :, part],
+                    corners.at[0 if dx > 0 else 1, 1 - side, :, part],
                 ))
         return [
             pltpu.make_async_remote_copy(
@@ -136,35 +144,43 @@
 
     def place(field, strips, corners):
         for side in range(2):
-            span = pl.ds(BASE - WIDE if side == 0 else BASE + cells_y, WIDE)
-            field[:, WIDE:hi, span, :] = strips[side]
+            start = BASE - WIDE if side == 0 else BASE + cells_y
+            span = pl.ds(start, WIDE)
+            for c in range(3):
+                for j in range(WIDE):
+                    field[c, WIDE:hi, start + j, :] = strips[side, c, j]
             field[:, 0:WIDE, span, :] = corners[0, side]
             field[:, hi : hi + WIDE, span, :] = corners[1, side]
 
-    own = margins(dom, U, near, diag, send_sem, recv_sem)
-    inflow = margins(1, I, near_in, diag_in, in_send, in_recv)
+    to_pre = margins(0, U, near, diag, send_sem, recv_sem, WIDE - 1)
+    to_farm = margins(1, U, near, diag, send_sem, recv_sem, WIDE)
+    inflow = margins(1, I, near_in, diag_in, in_send, in_recv, WIDE - 1)
     block_in = pltpu.make_async_remote_copy(
         src_ref=U.at[:, pl.ds(WIDE, cells_x), inner, :],
         dst_ref=I.at[:, pl.ds(WIDE, cells_x), inner, :],
         send_sem=in_send.at[8], recv_sem=in_recv.at[8],
         device_id=(1 - dom, gx, gy), device_id_type=MESH,
     )
-    order = [4, 5, 6, 7, 2, 3, 0, 1]
-    for i in order:
-        own[i].start()
+    order = [2, 3, 4, 5, 6, 7, 0, 1]
 
     @pl.when(dom == 0)
     def _():
         for i in order:
+            to_pre[i].start()
+        for i in order:
             inflow[i].start()
         block_in.start()
-
-    for copy in own:
-        copy.wait_recv()
-    place(U, near, diag)
+        for copy in to_pre:
+            copy.wait_recv()
+        place(U, near, diag)
 
     @pl.when(dom == 1)
     def _():
+        for i in order:
+            to_farm[i].start()
+        for copy in to_farm:
+            copy.wait_recv()
+        place(U, near, diag)
         for copy in inflow:
             copy.wait_recv()
         block_in.wait_recv()
@@ -202,7 +218,7 @@
     def stage(field, result, margin, finish):
         starts = (BASE - margin, BASE + cells_y + margin - 8)
 
-        @pl.loop(WIDE - margin, hi + margin)
+        @pl.loop(WIDE - margin, hi + margin, unroll=cells_x + 2 * margin)
         def _(x):
             for row in starts:
                 centre, rates = rate(field, x, row)
@@ -290,12 +306,14 @@
             for i in range(1, count):
                 block_copy(i).wait_send()
 
-    for copy in own:
-        copy.wait_send()
+    @pl.when(dom == 1)
+    def _():
+        for copy in to_farm:
+            copy.wait_send()
 
     @pl.when(dom == 0)
     def _():
-        for copy in inflow:
+        for copy in to_pre + inflow:
             copy.wait_send()
         block_in.wait_send()
 
@@ -324,13 +342,13 @@
     fused = cells_y * depth == levels_z and 4 * total_y == levels_z and 8 * waves == levels_z
     sizes = (tiles_x, tiles_y, cells_x, cells_y, levels_z, fringe_len)
     field = pltpu.VMEM((3, cells_x + 2 * WIDE, cells_y + 2 * BASE, levels_z), jnp.float32)
-    strips = pltpu.VMEM((2, 3, cells_x, WIDE, levels_z), jnp.float32)
+    strips = pltpu.VMEM((2, 3, WIDE, cells_x, levels_z), jnp.float32)
     corners = pltpu.VMEM((2, 2, 3, WIDE, WIDE, levels_z), jnp.float32)
     dma = pltpu.SemaphoreType.DMA
-    scratch = [field] * 5 + [strips] * 3 + [corners] * 2
+    scratch = [field] * 5 + [strips] * 3 + [corners] * 3
     scratch += [pltpu.VMEM((cells_x + 2 * WIDE, levels_z), jnp.float32)]
     scratch += [dma, dma((8,)), dma((8,)), dma((9,)), dma((9,)), dma]
-    anywhere, vmem = pl.BlockSpec(memory_space=pl.ANY), pl.BlockSpec(memory_space=pltpu.VMEM)
+    anywhere, vmem = pl.BlockSpec(memory_space=pltpu.HBM), pl.BlockSpec(memory_space=pltpu.VMEM)
     args = [fringe_start, velocity]
     in_specs = [pl.BlockSpec(memory_space=pltpu.SMEM), anywhere]
     if fused:
@@ -345,7 +363,7 @@
             pltpu.VMEM((parts, cells_x, levels_z), jnp.float32),
             pltpu.VMEM((tiles_y, tiles_x, cells_x, levels_z), jnp.float32),
             pltpu.VMEM((tiles_y * levels_z, levels_z), jnp.float32),
-            dma((2,)), dma((parts * tiles_y,)), dma, dma,
+            dma((2,)), dma((parts * tiles_y,)), dma,
         ]
     else:
         second = (cells_x, cells_y, levels_z)
@@ -359,7 +377,7 @@
         out_specs=(anywhere, vmem),
         scratch_shapes=scratch,
         compiler_params=pltpu.CompilerParams(
-            collective_id=0, has_side_effects=True, vmem_limit_bytes=32 * 1024 * 1024
+            collective_id=0, has_side_effects=True, vmem_limit_bytes=60 * 1024 * 1024
         ),
         name="farm_step",
     )(*args)

time: 37 us -> 30.2 us (0.82)
  Pallas kernels: 31.5 us -> 26.4 us
  local copies, waits for them, and re-layouts: 3.97 us -> 2.37 us
    pallas_call x1, Pallas kernels: 31.5 us -> 26.4 us  [on_device(): pl.pallas_call(functools.partial(step_kernel, sizes, fused), out_shape=(j...]
    unnamed x8 -> x4, local copies, waits for them, and re-layouts: 3.97 us -> 2.37 us
where the time goes in v2:
time: 30.2 us; the launch traced here: 30 us
  Pallas kernels  26.4 us (87%)
  local copies, waits for them, and re-layouts  2.37 us (8%)
  between operations  1.29 us (4%)
    pallas_call x1, Pallas kernels, on_device(): pl.pallas_call(functools.partial(step_kernel, sizes, fused), out_shape=(j...  26.4 us
    unnamed x4, local copies, waits for them, and re-layouts  2.37 us

profile of v2, /device:TPU:1, one launch (start us, length us, event | category | flops | bytes accessed | tf_op | source)
XLA Modules:
  0.0 30.0 jit_solution(8360554584111686283)
XLA Ops:
  1.3 26.4 %farm_step.1 = (f32[1,3,16,8,128]{4,3,2,1,0:T(8,128)}, f32[2,16,16,32]{3,2,1,0:T(8,128)}) custom-call(s32[1]{0:T(128)S(6)} %copy.8.refs_0_, f32[1,3,16,8,128]{4,3,2,1,0:T(8,128)} %refs_1_.1, f32[4,128,64]{2,1,0:T(8,128)} %constant.4.clone.refs_2_, f32[32,128]{1,0:T(8,128)} %constant.5.clone.refs_3_), custom_call_target="tpu_custom_call" | custom-call | tf_op jit(solution)/shard_map/farm_step/pallas_call | solution.py:370
  27.7 0.0 copy-start
  27.7 1.7 %copy.9 = f32[1,3,16,8,128]{4,3,2,1,0:T(8,128)} copy(f32[1,3,16,8,128]{4,3,2,1,0:T(8,128)} %get-tuple-element.4) | data formatting | bytes 393216
  29.3 0.0 copy-done
  29.3 0.7 %copy.10 = f32[2,16,16,32]{3,2,1,0:T(8,128)} copy(f32[2,16,16,32]{3,2,1,0:T(8,128)S(1)} %copy-done) | data formatting | bytes 131072
Async XLA Ops:
  27.7 1.7 %copy-start = (f32[2,16,16,32]{3,2,1,0:T(8,128)S(1)}, f32[2,16,16,32]{3,2,1,0:T(8,128)}, u32[]{:S(2)}) copy-start(f32[2,16,16,32]{3,2,1,0:T(8,128)} %get-tuple-element.5) | copy-start | bytes 196612

commit v3 on v2

--- a/solution.py
+++ b/solution.py
@@ -41,13 +41,13 @@
 def step_kernel(sizes, fused, *refs):
     tiles_x, tiles_y, cells_x, cells_y, levels_z, fringe_len = sizes
     if fused:
-        (fs_ref, u_hbm, tx_hbm, ty_hbm, v_hbm, spec_ref, *scratch) = refs
+        (fs_ref, u_hbm, v_hbm, got, *scratch) = refs
     else:
         (fs_ref, u_hbm, v_hbm, div_ref, *scratch) = refs
     (U, I, S1, S2, S3, edge, near, near_in, tips, diag, diag_in, ramp) = scratch[:12]
     (load_sem, send_sem, recv_sem, in_send, in_recv, out_sem) = scratch[12:18]
     if fused:
-        tx, ty, rows, block, got, turned, tab_sem, blk_send, blk_recv = scratch[18:]
+        rows, block, blk_send, blk_recv = scratch[18:]
     dom, gx, gy = (lax.axis_index(name) for name in ("dom", "gx", "gy"))
     count = 2 * tiles_x * tiles_y
     me = (dom * tiles_x + gx) * tiles_y + gy
@@ -87,11 +87,6 @@
 
     load = pltpu.make_async_copy(u_hbm.at[0], U.at[:, pl.ds(WIDE, cells_x), inner, :], load_sem)
     load.start()
-    if fused:
-        tab_x = pltpu.make_async_copy(tx_hbm.at[gy], tx, tab_sem.at[0])
-        tab_y = pltpu.make_async_copy(ty_hbm, ty, tab_sem.at[1])
-        tab_x.start()
-        tab_y.start()
 
     cell = lax.broadcasted_iota(jnp.int32, ramp.shape, 0) + (gx * cells_x - WIDE)
     offset = cell - fs_ref[0]
@@ -142,6 +137,28 @@
             for i, (source, target) in enumerate(pieces)
         ]
 
+    def onward(width):
+        less = width - 1
+        pairs = []
+        for dx, dy in around:
+            side = 0 if dy > 0 else 1
+            span = pl.ds(WIDE - width if dy > 0 else 0, width)
+            slab = pl.ds(WIDE - width if dx > 0 else hi, width)
+            part = (0 if dx > 0 else 1, side, slice(None), pl.ds(WIDE - less if dx > 0 else 0, less))
+            if dy == 0:
+                pairs.append((U.at[:, slab, inner, :], I.at[:, slab, inner, :]))
+            elif dx == 0:
+                pairs.append((near.at[side, :, span], near_in.at[side, :, span]))
+            else:
+                pairs.append((diag.at[part], diag_in.at[part]))
+        return [
+            pltpu.make_async_remote_copy(
+                src_ref=source, dst_ref=target, send_sem=in_send.at[i], recv_sem=in_recv.at[i],
+                device_id=(1 - dom, gx, gy), device_id_type=MESH,
+            )
+            for i, (source, target) in enumerate(pairs)
+        ]
+
     def place(field, strips, corners):
         for side in range(2):
             start = BASE - WIDE if side == 0 else BASE + cells_y
@@ -154,7 +171,7 @@
 
     to_pre = margins(0, U, near, diag, send_sem, recv_sem, WIDE - 1)
     to_farm = margins(1, U, near, diag, send_sem, recv_sem, WIDE)
-    inflow = margins(1, I, near_in, diag_in, in_send, in_recv, WIDE - 1)
+    inflow = onward(WIDE - 1)
     block_in = pltpu.make_async_remote_copy(
         src_ref=U.at[:, pl.ds(WIDE, cells_x), inner, :],
         dst_ref=I.at[:, pl.ds(WIDE, cells_x), inner, :],
@@ -167,11 +184,10 @@
     def _():
         for i in order:
             to_pre[i].start()
+        block_in.start()
         for i in order:
+            to_pre[i].wait_recv()
             inflow[i].start()
-        block_in.start()
-        for copy in to_pre:
-            copy.wait_recv()
         place(U, near, diag)
 
     @pl.when(dom == 1)
@@ -181,15 +197,11 @@
         for copy in to_farm:
             copy.wait_recv()
         place(U, near, diag)
-        for copy in inflow:
-            copy.wait_recv()
-        block_in.wait_recv()
-        place(I, near_in, diag_in)
 
     lane = lax.broadcasted_iota(jnp.int32, (8, levels_z), 1)
     first, last = lane == 0, lane == levels_z - 1
 
-    def rate(field, x, row):
+    def rate(field, x, row, pulled=True):
         centre = [field[c, x, pl.ds(row, 8), :] for c in range(3)]
         grads, laps = [[], [], []], []
         for c in range(3):
@@ -211,23 +223,42 @@
         rates = []
         for c in range(3):
             carried = centre[0] * grads[0][c] + centre[1] * grads[1][c] + centre[2] * grads[2][c]
-            behind = I[c, x, pl.ds(row, 8), :] - centre[c]
-            rates.append(eddy * laps[c] - 0.5 * carried + pull * behind)
+            free = eddy * laps[c] - 0.5 * carried
+            if pulled:
+                free = free + pull * (I[c, x, pl.ds(row, 8), :] - centre[c])
+            rates.append(free)
         return centre, rates
 
-    def stage(field, result, margin, finish):
+    def stage(field, result, margin, finish, pulled=True):
         starts = (BASE - margin, BASE + cells_y + margin - 8)
 
         @pl.loop(WIDE - margin, hi + margin, unroll=cells_x + 2 * margin)
         def _(x):
             for row in starts:
-                centre, rates = rate(field, x, row)
+                centre, rates = rate(field, x, row, pulled)
                 for c in range(3):
                     result[c, x, pl.ds(row, 8), :] = finish(
                         U[c, x, pl.ds(row, 8), :], centre[c] + time_step * rates[c]
                     )
 
-    stage(U, S1, 3, lambda start, moved: moved)
+    stage(U, S1, 3, lambda start, moved: moved, pulled=False)
+
+    @pl.when(dom == 1)
+    def _():
+        for copy in inflow:
+            copy.wait_recv()
+        block_in.wait_recv()
+        place(I, near_in, diag_in)
+
+        @pl.loop(WIDE - 3, hi + 3, unroll=2)
+        def _(x):
+            pull = time_step * jnp.broadcast_to(ramp[pl.ds(x, 1), :], (8, levels_z))
+            for row in (BASE - 3, BASE + 5):
+                for c in range(3):
+                    S1[c, x, pl.ds(row, 8), :] += pull * (
+                        I[c, x, pl.ds(row, 8), :] - U[c, x, pl.ds(row, 8), :]
+                    )
+
     stage(S1, S2, 2, lambda start, moved: 0.75 * start + 0.25 * moved)
     stage(S2, S3, 1, lambda start, moved: (1.0 / 3.0) * start + (2.0 / 3.0) * moved)
 
@@ -275,31 +306,7 @@
                 block_copy(i).start()
             pltpu.make_async_copy(block.at[me // tiles_y], got.at[gy, gx], blk_recv).start()
 
-        tab_x.wait()
-        tab_y.wait()
         pltpu.make_async_copy(got, got, blk_recv).wait()
-        highest = lax.Precision.HIGHEST
-        for g in range(tiles_y):
-            lines = got[g].reshape(total_x, levels_z)
-            partly = jnp.dot(tx[...], lines, precision=highest, preferred_element_type=jnp.float32)
-            turned[g * levels_z : (g + 1) * levels_z, :] = partly.T
-        total_y = cells_y * tiles_y
-        waves = total_x // tiles_y
-        wide = 2 * waves
-        each = levels_z // wide
-        chunk = lax.broadcasted_iota(jnp.int32, (total_y, levels_z), 1) // wide
-        for q in range(depth // each):
-            packed = None
-            for j in range(each):
-                level = turned[pl.ds(q * each + j, total_y, stride=depth), :]
-                packed = level if j == 0 else jnp.where(chunk == j, level, packed)
-            both = jnp.dot(packed.T, ty[...], precision=highest, preferred_element_type=jnp.float32)
-            for j in range(each):
-                real = both[j * wide : j * wide + waves]
-                imag = both[j * wide + waves : (j + 1) * wide]
-                whole = real + pltpu.roll(imag, 2 * total_y, 1)
-                spec_ref[0, q * each + j] = whole[:, :total_y]
-                spec_ref[1, q * each + j] = whole[:, total_y : 2 * total_y]
 
         @pl.when(dom == 1)
         def _():
@@ -318,6 +325,54 @@
         block_in.wait_send()
 
     out.wait()
+
+
+def transform_kernel(
+    sizes, got_hbm, tx_hbm, ty_hbm, v_from, v_hbm, spec_hbm, spec_ref, turned, got, tx, ty, v_ref, sems
+):
+    tiles_x, tiles_y, cells_x, cells_y, levels_z, _ = sizes
+    gy = lax.axis_index("gy")
+    total_x = cells_x * tiles_x
+    depth = levels_z // (2 * tiles_x)
+    loads = [
+        pltpu.make_async_copy(source, target, sems.at[i + 2])
+        for i, (source, target) in enumerate(
+            [(got_hbm, got), (tx_hbm.at[gy], tx), (ty_hbm, ty), (v_from, v_ref)]
+        )
+    ]
+    for load in loads:
+        load.start()
+    save = pltpu.make_async_copy(v_ref, v_hbm, sems.at[0])
+    for load in loads[:3]:
+        load.wait()
+    highest = lax.Precision.HIGHEST
+    for g in range(tiles_y):
+        lines = got[g].reshape(total_x, levels_z)
+        partly = jnp.dot(tx[...], lines, precision=highest, preferred_element_type=jnp.float32)
+        turned[g * levels_z : (g + 1) * levels_z, :] = partly.T
+    total_y = cells_y * tiles_y
+    waves = total_x // tiles_y
+    wide = 2 * waves
+    each = levels_z // wide
+    chunk = lax.broadcasted_iota(jnp.int32, (total_y, levels_z), 1) // wide
+    loads[3].wait()
+    save.start()
+    for q in range(depth // each):
+        packed = None
+        for j in range(each):
+            level = turned[pl.ds(q * each + j, total_y, stride=depth), :]
+            packed = level if j == 0 else jnp.where(chunk == j, level, packed)
+        both = jnp.dot(packed.T, ty[...], precision=highest, preferred_element_type=jnp.float32)
+        for j in range(each):
+            real = both[j * wide : j * wide + waves]
+            imag = both[j * wide + waves : (j + 1) * wide]
+            whole = real + pltpu.roll(imag, 2 * total_y, 1)
+            spec_ref[0, q * each + j] = whole[:, :total_y]
+            spec_ref[1, q * each + j] = whole[:, total_y : 2 * total_y]
+    store = pltpu.make_async_copy(spec_ref, spec_hbm, sems.at[1])
+    store.start()
+    store.wait()
+    save.wait()
 
 
 def tables(tiles_y, total_x, total_y, each):
@@ -352,18 +407,11 @@
     args = [fringe_start, velocity]
     in_specs = [pl.BlockSpec(memory_space=pltpu.SMEM), anywhere]
     if fused:
-        along, across = tables(tiles_y, total_x, total_y, levels_z // (2 * waves))
-        args += [jnp.asarray(along), jnp.asarray(across)]
-        in_specs += [anywhere, anywhere]
-        second = (2, depth, waves, total_y)
+        second = (tiles_y, tiles_x, cells_x, levels_z)
         scratch += [
-            pltpu.VMEM(along.shape[1:], jnp.float32),
-            pltpu.VMEM(across.shape, jnp.float32),
             pltpu.VMEM((cells_x * cells_y, levels_z), jnp.float32),
             pltpu.VMEM((parts, cells_x, levels_z), jnp.float32),
-            pltpu.VMEM((tiles_y, tiles_x, cells_x, levels_z), jnp.float32),
-            pltpu.VMEM((tiles_y * levels_z, levels_z), jnp.float32),
-            dma((2,)), dma((parts * tiles_y,)), dma,
+            dma((parts * tiles_y,)), dma,
         ]
     else:
         second = (cells_x, cells_y, levels_z)
@@ -382,7 +430,28 @@
         name="farm_step",
     )(*args)
     if fused:
-        return field_out, other
+        along, across = tables(tiles_y, total_x, total_y, levels_z // (2 * waves))
+        result = (2, depth, waves, total_y)
+        return pl.pallas_call(
+            functools.partial(transform_kernel, sizes),
+            out_shape=(
+                jax.ShapeDtypeStruct(velocity.shape, jnp.float32),
+                jax.ShapeDtypeStruct(result, jnp.float32),
+            ),
+            in_specs=[anywhere] * 4,
+            out_specs=(anywhere, anywhere),
+            scratch_shapes=[
+                pltpu.VMEM(result, jnp.float32),
+                pltpu.VMEM((tiles_y * levels_z, levels_z), jnp.float32),
+                pltpu.VMEM(second, jnp.float32),
+                pltpu.VMEM(along.shape[1:], jnp.float32),
+                pltpu.VMEM(across.shape, jnp.float32),
+                pltpu.VMEM(velocity.shape, jnp.float32),
+                dma((6,)),
+            ],
+            compiler_params=pltpu.CompilerParams(vmem_limit_bytes=60 * 1024 * 1024),
+            name="transform",
+        )(other, jnp.asarray(along), jnp.asarray(across), field_out)
     return field_out, spectrum_of(other)
 
 

time: 30.2 us -> 28.4 us (0.940)
  local copies, waits for them, and re-layouts: 2.37 us -> 0 us
  Pallas kernels: 26.4 us -> 26.9 us
    pallas_call x0 -> x1, Pallas kernels: none -> 2.69 us  [on_device(): pl.pallas_call(functools.partial(transform_kernel, sizes), out_shape=(jax...]
    unnamed x4 -> x0, local copies, waits for them, and re-layouts: 2.37 us -> none
    pallas_call x1, Pallas kernels: 26.4 us -> 24.3 us  [on_device(): pl.pallas_call(functools.partial(step_kernel, sizes, fused), out_shape=(j...]
where the time goes in v3:
time: 28.4 us; the launch traced here: 28.2 us
  Pallas kernels  26.9 us (95%)
  between operations  1.28 us (5%)
    pallas_call x1, Pallas kernels, on_device(): pl.pallas_call(functools.partial(step_kernel, sizes, fused), out_shape=(j...  24.3 us
    pallas_call x1, Pallas kernels, on_device(): pl.pallas_call(functools.partial(transform_kernel, sizes), out_shape=(jax...  2.69 us

profile of v3, /device:TPU:1, one launch (start us, length us, event | category | flops | bytes accessed | tf_op | source)
XLA Modules:
  0.0 28.2 jit_solution(14921744611805379694)
XLA Ops:
  1.3 24.3 %farm_step.1 = (f32[1,3,16,8,128]{4,3,2,1,0:T(8,128)}, f32[4,4,16,128]{3,2,1,0:T(8,128)}) custom-call(s32[1]{0:T(128)S(6)} %copy.6.refs_0_, f32[1,3,16,8,128]{4,3,2,1,0:T(8,128)} %refs_1_.1), custom_call_target="tpu_custom_call" | custom-call | tf_op jit(solution)/shard_map/farm_step/pallas_call | solution.py:418
  25.5 2.7 %transform.1 = (f32[1,3,16,8,128]{4,3,2,1,0:T(8,128)}, f32[2,16,16,32]{3,2,1,0:T(8,128)}) custom-call(f32[4,4,16,128]{3,2,1,0:T(8,128)} %get-tuple-element.4.got_hbm, f32[4,128,64]{2,1,0:T(8,128)} %constant.4.clone.tx_hbm, f32[32,128]{1,0:T(8,128)} %constant.5.clone.ty_hbm, f32[1,3,16,8,128]{4,3,2,1,0:T(8,128)} %get-tuple-element.5.v_from), custom_call_target="tpu_custom_call" | custom-call | tf_op jit(solution)/shard_map/transform/pallas_call | solution.py:435

commit v4 on v3

--- a/solution.py
+++ b/solution.py
@@ -178,7 +178,7 @@
         send_sem=in_send.at[8], recv_sem=in_recv.at[8],
         device_id=(1 - dom, gx, gy), device_id_type=MESH,
     )
-    order = [2, 3, 4, 5, 6, 7, 0, 1]
+    order = [4, 5, 6, 7, 2, 3, 0, 1]
 
     @pl.when(dom == 0)
     def _():

time: 28.4 us -> 27.5 us (0.968)
  Pallas kernels: 26.9 us -> 26 us
    pallas_call x1, Pallas kernels: 24.3 us -> 23.3 us  [on_device(): pl.pallas_call(functools.partial(step_kernel, sizes, fused), out_shape=(j...]
where the time goes in v4:
time: 27.5 us; the launch traced here: 27.3 us
  Pallas kernels  26 us (95%)
  between operations  1.28 us (5%)
    pallas_call x1, Pallas kernels, on_device(): pl.pallas_call(functools.partial(step_kernel, sizes, fused), out_shape=(j...  23.3 us
    pallas_call x1, Pallas kernels, on_device(): pl.pallas_call(functools.partial(transform_kernel, sizes), out_shape=(jax...  2.69 us

profile of v4, /device:TPU:1, one launch (start us, length us, event | category | flops | bytes accessed | tf_op | source)
XLA Modules:
  0.0 27.3 jit_solution(9097031472162268657)
XLA Ops:
  1.3 23.3 %farm_step.1 = (f32[1,3,16,8,128]{4,3,2,1,0:T(8,128)}, f32[4,4,16,128]{3,2,1,0:T(8,128)}) custom-call(s32[1]{0:T(128)S(6)} %copy.6.refs_0_, f32[1,3,16,8,128]{4,3,2,1,0:T(8,128)} %refs_1_.1), custom_call_target="tpu_custom_call" | custom-call | tf_op jit(solution)/shard_map/farm_step/pallas_call | solution.py:418
  24.6 2.7 %transform.1 = (f32[1,3,16,8,128]{4,3,2,1,0:T(8,128)}, f32[2,16,16,32]{3,2,1,0:T(8,128)}) custom-call(f32[4,4,16,128]{3,2,1,0:T(8,128)} %get-tuple-element.4.got_hbm, f32[4,128,64]{2,1,0:T(8,128)} %constant.4.clone.tx_hbm, f32[32,128]{1,0:T(8,128)} %constant.5.clone.ty_hbm, f32[1,3,16,8,128]{4,3,2,1,0:T(8,128)} %get-tuple-element.5.v_from), custom_call_target="tpu_custom_call" | custom-call | tf_op jit(solution)/shard_map/transform/pallas_call | solution.py:435
